TPU v7x, 128 devices: a whole 4x4x4 slice. The times are simulated.
128 devices in a mesh: dp: 16 (over z, y_lo, core), mp: 8 (over x, y_hi).
Axes of the slice: x: 4, y: 4 (y_hi: 2, y_lo: 2; y = y_hi * 2 + y_lo), z: 4, core: 2. Of those that a mesh axis runs over, the one named last changes fastest.
Arguments:
- tokens: float32 [20480, 1152], P(('dp', 'mp')), may hold values from -6 to 6
- cotangent: float32 [20480, 1152], P(('dp', 'mp')), may hold values from -6 to 6
- time_embed: float32 [32, 1152], replicated, may hold values from -6 to 6
- attend_weight: bfloat16 [1, 3, 1152, 1152], P(None, None, 'dp', 'mp'), may hold values from -0.1875 to 0.1875
- time_weight: bfloat16 [1, 2, 1152, 1152], P(None, None, 'dp', 'mp'), may hold values from -0.1875 to 0.1875
- out_weight: bfloat16 [1, 1152, 1152], P(None, 'mp', 'dp'), may hold values from -0.75 to 0.75
- expand_weight: bfloat16 [1, 4608, 1152], P(None, 'mp', 'dp'), may hold values from -0.1875 to 0.1875
- reduce_weight: bfloat16 [1, 4608, 1152], P(None, 'mp', 'dp'), may hold values from -0.09375 to 0.09375
- row_params: bfloat16 [1, 6, 1152], P(None, None, 'dp')
- expand_bias: float32 [1, 4608], P(None, 'mp'), may hold values from -3 to 3
- bias_table: float32 [1, 16, 1521], P(None, 'mp'), may hold values from -4 to 4
- grid_height: int32 [64], P('dp'), may hold values from 12 to 20, as said below
- grid_width: int32 [64], P('dp'), may hold values from 12 to 20
- group_count: int32 [16], P('dp'), may hold values from 1 to 4, as said below
- group_bucket: int32 [16], P('dp'), may hold values from 0 to 31
- shares: int32 [16], replicated, may hold values from 1 to 8
Outputs:
- output: float32 [20480, 1152], P(('dp', 'mp'))
- grad_tokens: float32 [20480, 1152], P(('dp', 'mp'))
- grad_attend: float32 [1, 3, 1152, 1152], P(None, None, 'dp', 'mp')
- grad_time: float32 [1, 2, 1152, 1152], P(None, None, 'dp', 'mp')
- grad_out: float32 [1, 1152, 1152], P(None, 'mp', 'dp')
- grad_expand: float32 [1, 4608, 1152], P(None, 'mp', 'dp')
- grad_reduce: float32 [1, 4608, 1152], P(None, 'mp', 'dp')
- grad_rows: float32 [1, 6, 1152], P(None, None, 'dp')
- grad_expand_bias: float32 [1, 4608], P(None, 'mp')
- grad_table: float32 [1, 16, 1521], P(None, 'mp')
Inputs may be any that keep to these rules, and one draw needn't show every extreme that they name: Each image's grid_height * grid_width lies between 192 and 320; some image has height 12 and some height 20. `group_count`: some group is full.
All inputs are finite; a program needn't handle non-finite values.
Results may differ from a plain program's by a relative error of at most 0.025.
Values may be sent and summed in bfloat16 or wider, within the bound.
A program may use at most 448 MiB of HBM per device.

v0:
```python
from functools import partial

import jax
import jax.numpy as jnp
from jax import lax
from jax.sharding import Mesh
from jax.sharding import PartitionSpec as P

HEAD_DIM = 72
LAYERS = 1
SLOTS = 4
PAD = 320
GRID_MAX = 20
MP = ("mp_0", "mp_1")
DP_MP = ("dp", "mp_0", "mp_1")


EPSILON = 1e-06
MASKED = -1e30


def gathered_by_axis(x, axes, dim):
    if not axes:
        return x
    nearer = lax.all_gather(x, axes[-1], axis=dim, tiled=True)
    return gathered_by_axis(nearer, axes[:-1], dim)


def summed_rows(terms, axes):
    subtotal = terms.astype(jnp.bfloat16)
    for axis in axes:
        subtotal = lax.psum_scatter(subtotal, axis, scatter_dimension=0, tiled=True)
    return subtotal.astype(jnp.float32)


def gather_turned(arrays, axis, dims):
    turned = [jnp.moveaxis(a, dim, 0) for a, dim in zip(arrays, dims)]
    widths = [t[0].size for t in turned]
    both = jnp.concatenate([t.reshape(-1, w) for t, w in zip(turned, widths)], axis=1)
    filled = lax.all_gather(both, axis, axis=0, tiled=True)
    pieces = jnp.split(filled, [sum(widths[:k]) for k in range(1, len(widths))], axis=1)
    return tuple(
        (
            jnp.moveaxis(b.reshape(-1, *t.shape[1:]), 0, dim)
            for b, t, dim in zip(pieces, turned, dims)
        )
    )


def in_one_piece(arrays, axis, dim, along):
    both = jnp.concatenate(arrays, axis=along)
    filled, at, finished = (lax.psum_scatter(both, axis, scatter_dimension=dim, tiled=True), 0, [])
    for a in arrays:
        finished.append(lax.slice_in_dim(filled, at, at + a.shape[along], axis=along))
        at += a.shape[along]
    return tuple(finished)


def sent_to_all(x, axis):
    count = lax.axis_size(axis)
    return lax.all_to_all(jnp.broadcast_to(x[None], (count, *x.shape)), axis, 0, 0, tiled=True)


def taken_together(x, axis):
    return sent_to_all(x, axis).sum(axis=0)


def together(arrays, axis):
    ends = [0]
    for a in arrays:
        ends.append(ends[-1] + a.size)
    subtotal = taken_together(jnp.concatenate([a.ravel() for a in arrays]), axis)
    return tuple((subtotal[b:e].reshape(a.shape) for a, b, e in zip(arrays, ends, ends[1:])))


def layer_norm(values, norm_gain, offset):
    row_mean = jnp.mean(values, axis=-1, keepdims=True)
    centred = values - row_mean
    spread = jnp.mean(centred * centred, axis=-1, keepdims=True)
    return centred * lax.rsqrt(spread + EPSILON) * norm_gain + offset


def gelu_tanh(values):
    return jax.nn.gelu(values, approximate=True)


def grid_index(height, grid_width):
    position = jnp.arange(PAD, dtype=jnp.int32)
    grid_row = position // grid_width
    grid_col = position % grid_width
    side = 2 * GRID_MAX - 1
    rel_index = (grid_row[:, None] - grid_row[None, :] + (GRID_MAX - 1)) * side + (
        grid_col[:, None] - grid_col[None, :] + (GRID_MAX - 1)
    )
    return jnp.clip(rel_index, 0, side * side - 1)


def gather_rows(block):
    return gathered_by_axis(block, MP, 0)


def spread_sum(term_fn, own_rows):
    return summed_rows(term_fn(jnp.int32(0), own_rows * lax.axis_size(MP)), MP)


def layer_weights(
    attend_weight, time_weight, out_weight, expand_weight, reduce_weight, row_params, layer_pos
):
    return gather_turned(
        (
            attend_weight[layer_pos],
            time_weight[layer_pos],
            out_weight[layer_pos],
            expand_weight[layer_pos],
            reduce_weight[layer_pos],
            row_params[layer_pos],
        ),
        "dp",
        (1, 1, 1, 1, 1, 1),
    )


def rows_product(left, right, first_row, row_count):
    return jnp.dot(left, right, preferred_element_type=jnp.float32)


def triple_product(triple, weights, first_row, row_count):
    return jnp.einsum("cre,cde->rd", triple, weights, preferred_element_type=jnp.float32)


def project(full_rows, attend_mat, time_mat, time_low):
    projected = jnp.einsum("rd,cde->cre", full_rows, attend_mat, preferred_element_type=jnp.float32)
    query_bias = jnp.dot(time_low[None, :], time_mat[0], preferred_element_type=jnp.float32)
    value_bias = jnp.dot(time_low[None, :], time_mat[1], preferred_element_type=jnp.float32)
    queries = (projected[0] + query_bias).astype(jnp.bfloat16)
    return (
        queries,
        projected[1].astype(jnp.bfloat16),
        projected[2].astype(jnp.bfloat16),
        value_bias,
    )


def position_bias(table, rel_index):
    return jnp.transpose(jnp.take(table, rel_index, axis=1), (1, 0, 2, 3))


def score_block(queries, key_rows, bias4, key_valid):
    shape4 = (SLOTS, PAD, bias4.shape[1], HEAD_DIM)
    scores = jnp.einsum(
        "sqhe,skhe->shqk",
        queries.reshape(shape4),
        key_rows.reshape(shape4),
        preferred_element_type=jnp.float32,
    ) * HEAD_DIM ** (-0.5)
    scores = scores + bias4
    return jnp.where(key_valid[:, None, None, :], scores, MASKED)


def mix_values(weights_low, values, value_bias):
    shape4 = (SLOTS, PAD, values.shape[1] // HEAD_DIM, HEAD_DIM)
    mixed = jnp.einsum(
        "shqk,skhe->sqhe", weights_low, values.reshape(shape4), preferred_element_type=jnp.float32
    )
    return (mixed.reshape(values.shape) + value_bias).astype(jnp.bfloat16)


def body(
    tokens,
    cotangent,
    time_embed,
    attend_weight,
    time_weight,
    out_weight,
    expand_weight,
    reduce_weight,
    row_params,
    expand_bias,
    bias_table,
    grid_height,
    grid_width,
    group_count,
    group_bucket,
    shares,
):
    own_rows = tokens.shape[0]
    total_rows = SLOTS * PAD
    first_own = lax.axis_index(MP) * own_rows
    slot_ids = jnp.arange(SLOTS, dtype=jnp.int32)
    lengths = grid_height * grid_width * (slot_ids < group_count[0]).astype(jnp.int32)
    key_valid = jnp.arange(PAD, dtype=jnp.int32)[None, :] < lengths[:, None]
    valid_own = lax.dynamic_slice_in_dim(
        key_valid.reshape(total_rows).astype(jnp.float32), first_own, own_rows, 0
    )
    rel_index = jax.vmap(grid_index)(grid_height, grid_width)
    flat_index = rel_index.reshape(-1)
    side = 2 * GRID_MAX - 1
    time_low = lax.dynamic_index_in_dim(time_embed, group_bucket[0], 0, keepdims=False).astype(
        jnp.bfloat16
    )
    time_f = time_low.astype(jnp.float32)
    share_f = shares.astype(jnp.float32)
    weight = share_f[lax.axis_index("dp")] * share_f.shape[0] / jnp.sum(share_f)
    residual = tokens
    kept_weights = []
    layer_pos = 0
    gathered = layer_weights(
        attend_weight, time_weight, out_weight, expand_weight, reduce_weight, row_params, layer_pos
    )
    kept_weights.append(gathered)
    attend_mat, time_mat, out_mat, expand_mat, reduce_mat, rows_mat = gathered
    rows_f = rows_mat.astype(jnp.float32)
    inputs_kept = [residual]
    normed = layer_norm(residual, rows_f[0], rows_f[1]).astype(jnp.bfloat16)
    full_rows = gather_rows(normed)
    queries, key_rows, values, value_bias = project(full_rows, attend_mat, time_mat, time_low)
    bias4 = position_bias(bias_table[layer_pos], rel_index)
    bias_kept = [bias4]
    scores = score_block(queries, key_rows, bias4, key_valid)
    top_score = jnp.max(scores, axis=-1, keepdims=True)
    exponent = jnp.exp(scores - top_score)
    row_total = jnp.sum(exponent, axis=-1, keepdims=True)
    lse_kept = [top_score + jnp.log(row_total)]
    mixed = mix_values((exponent / row_total).astype(jnp.bfloat16), values, value_bias)
    residual = residual + spread_sum(partial(rows_product, mixed, out_mat), own_rows) + rows_f[2]
    middles_kept = [residual]
    normed = layer_norm(residual, rows_f[3], rows_f[4]).astype(jnp.bfloat16)
    full_rows = gather_rows(normed)
    hidden = (
        jnp.einsum("rd,fd->rf", full_rows, expand_mat, preferred_element_type=jnp.float32)
        + expand_bias[layer_pos]
    )
    activated = gelu_tanh(hidden).astype(jnp.bfloat16)
    residual = (
        residual + spread_sum(partial(rows_product, activated, reduce_mat), own_rows) + rows_f[5]
    )
    output = residual * valid_own[:, None]
    grad_residual = cotangent * weight * valid_own[:, None]
    results = []
    for layer_pos in reversed(range(LAYERS)):
        gathered = layer_weights(
            attend_weight,
            time_weight,
            out_weight,
            expand_weight,
            reduce_weight,
            row_params,
            layer_pos,
        )
        attend_mat, time_mat, out_mat, expand_mat, reduce_mat, rows_mat = gathered
        rows_f = rows_mat.astype(jnp.float32)
        normed_f, norm_back = jax.vjp(layer_norm, middles_kept[layer_pos], rows_f[3], rows_f[4])
        full_rows = gather_rows(normed_f.astype(jnp.bfloat16))
        hidden = (
            jnp.einsum("rd,fd->rf", full_rows, expand_mat, preferred_element_type=jnp.float32)
            + expand_bias[layer_pos]
        )
        activated_f, gelu_back = jax.vjp(gelu_tanh, hidden)
        activated = activated_f.astype(jnp.bfloat16)
        grad_full = gather_rows(grad_residual.astype(jnp.bfloat16))
        bias_two = jnp.sum(grad_full.astype(jnp.float32), axis=0)
        grad_reduce = jnp.einsum(
            "rf,rd->fd", activated, grad_full, preferred_element_type=jnp.float32
        )
        grad_active = jnp.einsum(
            "rd,fd->rf", grad_full, reduce_mat, preferred_element_type=jnp.float32
        )
        grad_hidden = gelu_back(grad_active)[0].astype(jnp.bfloat16)
        grad_expand_bias = jnp.sum(grad_hidden.astype(jnp.float32), axis=0)
        grad_expand = jnp.einsum(
            "rf,rd->fd", grad_hidden, full_rows, preferred_element_type=jnp.float32
        )
        grad_normed = spread_sum(partial(rows_product, grad_hidden, expand_mat), own_rows)
        grad_middle, gain_two, offset_two = norm_back(grad_normed)
        grad_middle = grad_middle + grad_residual
        normed_f, norm_back = jax.vjp(layer_norm, inputs_kept[layer_pos], rows_f[0], rows_f[1])
        full_rows = gather_rows(normed_f.astype(jnp.bfloat16))
        queries, key_rows, values, value_bias = project(full_rows, attend_mat, time_mat, time_low)
        scores = score_block(queries, key_rows, bias_kept[layer_pos], key_valid)
        probs = jnp.exp(scores - lse_kept[layer_pos])
        weights_low = probs.astype(jnp.bfloat16)
        mixed = mix_values(weights_low, values, value_bias)
        grad_full = gather_rows(grad_middle.astype(jnp.bfloat16))
        bias_out = jnp.sum(grad_full.astype(jnp.float32), axis=0)
        grad_out = jnp.einsum("re,rd->ed", mixed, grad_full, preferred_element_type=jnp.float32)
        grad_mixed = jnp.einsum(
            "rd,ed->re", grad_full, out_mat, preferred_element_type=jnp.float32
        ).astype(jnp.bfloat16)
        shape4 = (SLOTS, PAD, values.shape[1] // HEAD_DIM, HEAD_DIM)
        grad_mixed4 = grad_mixed.reshape(shape4)
        grad_probs = jnp.einsum(
            "sqhe,skhe->shqk",
            grad_mixed4,
            values.reshape(shape4),
            preferred_element_type=jnp.float32,
        )
        grad_scores = probs * (grad_probs - jnp.sum(grad_probs * probs, axis=-1, keepdims=True))
        grad_scores = jnp.where(key_valid[:, None, None, :], grad_scores, 0.0).astype(jnp.bfloat16)
        grad_table = jax.vmap(
            lambda plane: jax.ops.segment_sum(
                plane.reshape(-1), flat_index, num_segments=side * side
            ),
            in_axes=1,
        )(grad_scores.astype(jnp.float32))
        scale = HEAD_DIM ** (-0.5)
        grad_queries = (
            (
                jnp.einsum(
                    "shqk,skhe->sqhe",
                    grad_scores,
                    key_rows.reshape(shape4),
                    preferred_element_type=jnp.float32,
                )
                * scale
            )
            .astype(jnp.bfloat16)
            .reshape(values.shape)
        )
        grad_keys = (
            (
                jnp.einsum(
                    "shqk,sqhe->skhe",
                    grad_scores,
                    queries.reshape(shape4),
                    preferred_element_type=jnp.float32,
                )
                * scale
            )
            .astype(jnp.bfloat16)
            .reshape(values.shape)
        )
        grad_values = (
            jnp.einsum(
                "shqk,sqhe->skhe", weights_low, grad_mixed4, preferred_element_type=jnp.float32
            )
            .astype(jnp.bfloat16)
            .reshape(values.shape)
        )
        grad_triple = jnp.stack([grad_queries, grad_keys, grad_values])
        grad_attend = jnp.einsum(
            "rd,cre->cde", full_rows, grad_triple, preferred_element_type=jnp.float32
        )
        grad_time = jnp.stack(
            [
                time_f[:, None] * jnp.sum(grad_queries.astype(jnp.float32), axis=0)[None, :],
                time_f[:, None] * jnp.sum(grad_mixed.astype(jnp.float32), axis=0)[None, :],
            ]
        )
        grad_normed = spread_sum(partial(triple_product, grad_triple, attend_mat), own_rows)
        grad_input, gain_one, offset_one = norm_back(grad_normed)
        grad_residual = grad_input + grad_middle
        norm_sums = lax.psum(jnp.stack([gain_one, offset_one, gain_two, offset_two]), MP)
        rows_grad = jnp.stack(
            [norm_sums[0], norm_sums[1], bias_out, norm_sums[2], norm_sums[3], bias_two]
        )
        shards = (
            *tuple(
                (
                    part.astype(jnp.float32)
                    for part in in_one_piece(
                        (grad_attend.astype(jnp.bfloat16), grad_time.astype(jnp.bfloat16)),
                        "dp",
                        1,
                        0,
                    )
                )
            ),
            *tuple(
                (
                    part.astype(jnp.float32)
                    for part in in_one_piece(
                        (
                            grad_out.astype(jnp.bfloat16),
                            grad_expand.astype(jnp.bfloat16),
                            grad_reduce.astype(jnp.bfloat16),
                            rows_grad.astype(jnp.bfloat16),
                        ),
                        "dp",
                        1,
                        0,
                    )
                )
            ),
        )
        bias_sums = together((grad_expand_bias, grad_table), "dp")
        results.append(tuple(shards) + tuple(bias_sums))
    ordered = results[::-1]
    stacked = [jnp.stack([entry[member] for entry in ordered]) for member in range(8)]
    return (
        output,
        grad_residual,
        stacked[0],
        stacked[1],
        stacked[2],
        stacked[3],
        stacked[4],
        stacked[5],
        stacked[6],
        stacked[7],
    )


def solution(mesh):
    torus = Mesh(mesh.devices.reshape(mesh.shape["dp"], 4, 2), ("dp", "mp_0", "mp_1"))
    in_specs = (
        P(DP_MP, None),
        P(DP_MP, None),
        P(),
        P(None, None, "dp", MP),
        P(None, None, "dp", MP),
        P(None, MP, "dp"),
        P(None, MP, "dp"),
        P(None, MP, "dp"),
        P(None, None, "dp"),
        P(None, MP),
        P(None, MP, None),
        P("dp"),
        P("dp"),
        P("dp"),
        P("dp"),
        P(),
    )
    out_specs = (
        P(DP_MP, None),
        P(DP_MP, None),
        P(None, None, "dp", MP),
        P(None, None, "dp", MP),
        P(None, MP, "dp"),
        P(None, MP, "dp"),
        P(None, MP, "dp"),
        P(None, None, "dp"),
        P(None, MP),
        P(None, MP, None),
    )
    return jax.shard_map(body, mesh=torus, in_specs=in_specs, out_specs=out_specs, check_vma=False)
```

profile of v0, /device:TPU:1, one launch (start us, length us, event | category | flops | bytes accessed | tf_op | source)
XLA Modules:
  0.0 4385.1 jit_solution(15885647539965489522)
XLA Ops:
  19.6 35.8 all-gather.6.cloned.1.call-done
  59.2 12.2 all_gather.33
  73.6 1343.4 %gather_fusion = f32[409600,2]{1,0:T(8,128)} fusion(f32[2,1521]{0,1:T(8,128)S(1)} %bitcast.190, s32[409600]{0:T(1024)S(1)} %broadcast_clamp_fusion), kind=kCustom, calls=%fused_computation | custom fusion | bytes 8192000 | tf_op jit(solution)/shard_map/jit(_take)/gather | solution.py:145
  1416.9 126.6 %copy.170 = f32[4,320,320,2]{1,2,3,0:T(8,128)} copy(f32[4,320,320,2]{3,2,1,0:T(8,128)} %bitcast.28) | data formatting | bytes 6553600 | tf_op jit(solution)/shard_map/jit(_take)/gather | solution.py:145
  1572.3 37.3 reduce-scatter.13.cloned.1.call-done
  1610.1 22.5 reduce-scatter.15.cloned.1.call-done
  1634.3 11.7 all_gather.35
  1648.9 10.8 all_gather.37
  1659.9 24.5 all-gather.10.cloned.1.call-done
  1690.8 33.3 all-gather.12.cloned.1.call-done
  1724.1 7.4 convert_reduce_fusion
  1739.1 7.4 convolution_convert_fusion.1
  1746.6 29.5 reduce-scatter.21.cloned.1.call-done
  1776.1 38.7 reduce-scatter.17.cloned.1.call-done
  1814.9 23.1 reduce-scatter.23.cloned.1.call-done
  1839.3 21.4 reduce-scatter.19.cloned.1.call-done
  1864.0 11.7 all_gather.39
  1876.0 38.1 all-gather.14.cloned.1.call-done
  1934.4 36.9 reduce-scatter.25.cloned.1.call-done
  2011.7 33.1 psum.7
  2044.8 12.7 concatenate.17
  2079.6 90.3 %copy.188 = f32[409600,2]{1,0:T(8,128)} copy(f32[409600,2]{0,1:T(2,128)} %bitcast.192) | data formatting | bytes 6553600 | tf_op jit(solution)/shard_map/vmap()/reshape | solution.py:301
  2169.9 2166.6 %scatter_custom_fusion = f32[2,1521]{0,1:T(8,128)S(1)} fusion(s32[409600]{0:T(1024)} %reshape.658, f32[409600,2]{1,0:T(8,128)} %copy.188, f32[]{:T(128)} %constant.32.clone.1), kind=kCustom, calls=%fused_computation.112 | custom fusion | flops 819200 | bytes 12680 | tf_op jit(solution)/shard_map/vmap()/scatter-add | solution.py:300
  4337.8 20.9 all-to-all-start
  (240 shorter events, 170.7 us)
Async XLA Ops:
  7.2 1542.9 %copy-start = (f32[32,1152]{1,0:T(8,128)S(1)}, f32[32,1152]{1,0:T(8,128)}, u32[]{:S(2)}) copy-start(f32[32,1152]{1,0:T(8,128)} %param.18) | copy-start | bytes 442372
  7.2 48.3 %all-gather.6.cloned.1.call-start = ((), (), s32[]{:S(2)}) async-start(), calls=%async_computation.10 | async-start | bytes 5013504 | tf_op jit(solution)/shard_map/all_gather | solution.py:40
  13.0 1537.5 %all-gather.8.cloned.1.call-start = ((), (), s32[]{:S(2)}) async-start(), calls=%async_computation.11 | async-start | bytes 3686400 | tf_op jit(solution)/shard_map/all_gather | solution.py:25
  19.4 39.8 copy-start.21
  19.6 51.8 %copy-start.23 = (f32[160]{0:T(256)}, f32[160]{0:T(256)S(1)}, u32[]{:S(2)}) copy-start(f32[160]{0:T(256)S(1)} %fusion.85) | copy-start | bytes 1924
  71.4 1538.2 %reduce-scatter.13.cloned.1.call-start = ((), (), s32[]{:S(2)}) async-start(), calls=%async_computation.12 | async-start | bytes 3686400 | tf_op jit(solution)/shard_map/reduce_scatter | solution.py:32
  1572.3 60.4 %reduce-scatter.15.cloned.1.call-start = ((), (), s32[]{:S(2)}) async-start(), calls=%async_computation.13 | async-start | bytes 1105920 | tf_op jit(solution)/shard_map/reduce_scatter | solution.py:32
  1609.6 39.2 copy-start.5
  1609.7 74.7 %all-gather.10.cloned.1.call-start = ((), (), s32[]{:S(2)}) async-start(), calls=%async_computation.14 | async-start | bytes 3686400 | tf_op jit(solution)/shard_map/all_gather | solution.py:25
  1646.1 78.0 %all-gather.12.cloned.1.call-start = ((), (), s32[]{:S(2)}) async-start(), calls=%async_computation.17 | async-start | bytes 3686400 | tf_op jit(solution)/shard_map/all_gather | solution.py:25
  1659.8 116.3 %reduce-scatter.21.cloned.1.call-start = ((), (), s32[]{:S(2)}) async-start(), calls=%async_computation.18 | async-start | bytes 3686400 | tf_op jit(solution)/shard_map/reduce_scatter | solution.py:32
  1739.1 75.8 %reduce-scatter.17.cloned.1.call-start = ((), (), s32[]{:S(2)}) async-start(), calls=%async_computation.15 | async-start | bytes 3686400 | tf_op jit(solution)/shard_map/reduce_scatter | solution.py:32
  1746.5 91.5 %reduce-scatter.23.cloned.1.call-start = ((), (), s32[]{:S(2)}) async-start(), calls=%async_computation.19 | async-start | bytes 1105920 | tf_op jit(solution)/shard_map/reduce_scatter | solution.py:32
  1776.1 84.7 %reduce-scatter.19.cloned.1.call-start = ((), (), s32[]{:S(2)}) async-start(), calls=%async_computation.16 | async-start | bytes 1105920 | tf_op jit(solution)/shard_map/reduce_scatter | solution.py:32
  1814.9 99.2 %all-gather.14.cloned.1.call-start = ((), (), s32[]{:S(2)}) async-start(), calls=%async_computation.20 | async-start | bytes 3686400 | tf_op jit(solution)/shard_map/all_gather | solution.py:25
  1875.7 42.3 copy-start.12
  1875.7 95.6 %reduce-scatter.25.cloned.1.call-start = ((), (), s32[]{:S(2)}) async-start(), calls=%async_computation.21 | async-start | bytes 3686400 | tf_op jit(solution)/shard_map/reduce_scatter | solution.py:32
  1934.3 73.9 %reduce-scatter.27.cloned.1.call-start = ((), (), s32[]{:S(2)}) async-start(), calls=%async_computation.22 | async-start | bytes 1105920 | tf_op jit(solution)/shard_map/reduce_scatter | solution.py:32
  1971.3 2395.9 %reduce-scatter.29.cloned.1.call-start = ((), (), s32[]{:S(2)}) async-start(), calls=%async_computation.23 | async-start | bytes 1880064
  1987.6 2384.9 %all-reduce.3.cloned.1.call-start = ((), (), s32[]{:S(2)}) async-start(), calls=%async_computation.24 | async-start | bytes 6008832
  2169.9 2201.3 %copy-start.6 = (f32[160,1152]{1,0:T(8,128)S(1)}, f32[160,1152]{1,0:T(8,128)}, u32[]{:S(2)}) copy-start(f32[160,1152]{1,0:T(8,128)} %param.17) | copy-start | bytes 2211844
  2169.9 2201.3 %copy-start.8 = (f32[160,1152]{1,0:T(8,128)S(1)}, f32[160,1152]{1,0:T(8,128)}, u32[]{:S(2)}) copy-start(f32[160,1152]{1,0:T(8,128)} %copy-done.7) | copy-start | bytes 2211844
  2169.9 2201.3 %copy-start.15 = (bf16[160,1152]{1,0:T(8,128)(2,1)S(1)}, bf16[160,1152]{1,0:T(8,128)(2,1)}, u32[]{:S(2)}) copy-start(bf16[160,1152]{1,0:T(8,128)(2,1)} %reduce-scatter.27.cloned.1.call-done) | copy-start | bytes 1105924
  4337.8 27.9 all-to-all-start
  (25 other events, 267.3 us)
Sparse Core Ops, SparseCore 0:
  13.2 42.2 all-gather.5
  71.5 38.4 all-gather.7
  1572.4 37.1 reduce-scatter.12
  1612.0 20.6 reduce-scatter.14
  1646.2 38.1 all-gather.9
  1686.0 38.0 all-gather.11
  1739.2 36.8 reduce-scatter.20
  1778.5 36.3 reduce-scatter.16
  1817.4 20.5 reduce-scatter.22
  1840.4 20.3 reduce-scatter.18
  1875.9 38.1 all-gather.13
  1934.4 36.8 reduce-scatter.24
  1973.7 20.6 reduce-scatter.26
  1996.6 59.9 reduce-scatter.28
  2059.1 130.3 all-reduce.2
where the time goes:
time: 4400 us; the launch traced here: 4390 us
  other arithmetic  2200 us (50%)
  local copies, waits for them, and re-layouts  1640 us (37%)
  waiting for transfers between devices  347 us (8%)
  blocking collectives  79.6 us (2%)
  matrix products  75.1 us (2%)
    scatter-add x1, other arithmetic, body(): jax.ops.segment_sum(plane.reshape(-1), flat_index, num_segments=side * side)  2170 us
    gather x2, local copies, waits for them, and re-layouts, position_bias(): return jnp.transpose(jnp.take(table, rel_index, axis=1), (1, 0, 2, 3))  1470 us
    reduce_scatter x8, waiting for transfers between devices, summed_rows(): subtotal = lax.psum_scatter(subtotal, axis, scatter_dimension=0, tiled=True)  210 us
    reshape x3, local copies, waits for them, and re-layouts, body(): plane.reshape(-1)  103 us
    all_gather x4, waiting for transfers between devices, gathered_by_axis(): nearer = lax.all_gather(x, axes[-1], axis=dim, tiled=True)  95.9 us
  transfers between devices with their start and end apart: 16, of which 12 were waited for; matrix products, arithmetic and copies ran while one was open for 88% of the time, Pallas kernels for 0%

commit v1 on v0

--- a/solution.py
+++ b/solution.py
@@ -1,8 +1,11 @@
+import functools
 from functools import partial
 
 import jax
 import jax.numpy as jnp
 from jax import lax
+from jax.experimental import pallas as pl
+from jax.experimental.pallas import tpu as pltpu
 from jax.sharding import Mesh
 from jax.sharding import PartitionSpec as P
 
@@ -71,6 +74,122 @@
         ends.append(ends[-1] + a.size)
     subtotal = taken_together(jnp.concatenate([a.ravel() for a in arrays]), axis)
     return tuple((subtotal[b:e].reshape(a.shape) for a, b, e in zip(arrays, ends, ends[1:])))
+
+
+CELLS=400; SIDE=20; HD=72; SCALE=72**-0.5
+bf=jnp.bfloat16; f32=jnp.float32
+
+def cell_maps(h, w, live):
+    a=lax.broadcasted_iota(jnp.int32,(CELLS,PAD),0)
+    r=(a*3277)>>16
+    c=a-r*SIDE
+    ok=(r<h)&(c<w)&live
+    p=lax.broadcasted_iota(jnp.int32,(CELLS,PAD),1)
+    to_cells=jnp.where(ok&(r*w+c==p),1.0,0.0).astype(bf)
+    a=lax.broadcasted_iota(jnp.int32,(PAD,CELLS),1)
+    r=(a*3277)>>16
+    c=a-r*SIDE
+    ok=(r<h)&(c<w)&live
+    p=lax.broadcasted_iota(jnp.int32,(PAD,CELLS),0)
+    to_rows=jnp.where(ok&(r*w+c==p),1.0,0.0).astype(bf)
+    return to_cells,to_rows
+
+def key_mask(h,w,live):
+    a=lax.broadcasted_iota(jnp.int32,(1,CELLS),1)
+    r=(a*3277)>>16
+    c=a-r*SIDE
+    return jnp.where((r<h)&(c<w)&live,0.0,-1e30)
+
+def dotnt(a,b): return lax.dot_general(a,b,(((1,),(1,)),((),())),preferred_element_type=f32)
+def dottn(a,b): return lax.dot_general(a,b,(((0,),(0,)),((),())),preferred_element_type=f32)
+def dot(a,b): return jnp.dot(a,b,preferred_element_type=f32)
+
+def fwd_kernel(H, hw_ref, strip_ref, q_ref, k_ref, v_ref, o_ref, p_ref, b_ref):
+    s=pl.program_id(0)
+    @pl.when(s==0)
+    def _():
+        for hd in range(H):
+            for i in range(SIDE):
+                off=SIDE*(SIDE-1-i)
+                b_ref[hd,SIDE*i:SIDE*i+SIDE,:]=strip_ref[hd,:,off:off+CELLS]
+    h=hw_ref[0,s]; w=hw_ref[1,s]; live=hw_ref[2,s]>0
+    to_cells,to_rows=cell_maps(h,w,live)
+    mask=key_mask(h,w,live)
+    qg=dot(to_cells,q_ref[...]).astype(bf)
+    kg=dot(to_cells,k_ref[...]).astype(bf)
+    vg=dot(to_cells,v_ref[...]).astype(bf)
+    outs=[]
+    for hd in range(H):
+        sl=slice(hd*HD,hd*HD+HD)
+        sc=dotnt(qg[:,sl],kg[:,sl])*SCALE+b_ref[hd]+mask
+        m=jnp.max(sc,axis=-1,keepdims=True)
+        e=jnp.exp(sc-m)
+        p=(e*(1.0/jnp.sum(e,axis=-1,keepdims=True))).astype(bf)
+        p_ref[0,hd]=p
+        outs.append(dot(p,vg[:,sl]).astype(bf))
+    o_ref[...]=dot(to_rows,jnp.concatenate([o.astype(f32) for o in outs],axis=1).astype(bf))
+
+def attn_fwd(q,k,v,strip,hw):
+    S=hw.shape[1]; H=q.shape[1]//HD
+    spec=pl.BlockSpec((PAD,H*HD),lambda s:(s,0))
+    return pl.pallas_call(functools.partial(fwd_kernel,H),grid=(S,),
+        out_shape=(jax.ShapeDtypeStruct(q.shape,f32),jax.ShapeDtypeStruct((S,H,CELLS,CELLS),bf)),
+        in_specs=[pl.BlockSpec(memory_space=pltpu.SMEM),pl.BlockSpec(strip.shape,lambda s:(0,0,0)),spec,spec,spec],
+        out_specs=(spec,pl.BlockSpec((1,H,CELLS,CELLS),lambda s:(s,0,0,0))),
+        scratch_shapes=[pltpu.VMEM((H,CELLS,CELLS),f32)],
+        compiler_params=pltpu.CompilerParams(vmem_limit_bytes=48*2**20))(hw,strip,q,k,v)
+
+def bwd_kernel(H, hw_ref, p_ref, do_ref, q_ref, k_ref, v_ref, dq_ref, dk_ref, dv_ref, gs_ref, g_ref):
+    s=pl.program_id(0)
+    @pl.when(s==0)
+    def _():
+        g_ref[...]=jnp.zeros_like(g_ref)
+    h=hw_ref[0,s]; w=hw_ref[1,s]; live=hw_ref[2,s]>0
+    to_cells,to_rows=cell_maps(h,w,live)
+    qg=dot(to_cells,q_ref[...]).astype(bf)
+    kg=dot(to_cells,k_ref[...]).astype(bf)
+    vg=dot(to_cells,v_ref[...]).astype(bf)
+    dg=dot(to_cells,do_ref[...]).astype(bf)
+    dqs,dks,dvs=[],[],[]
+    for hd in range(H):
+        sl=slice(hd*HD,hd*HD+HD)
+        p=p_ref[0,hd]
+        pf=p.astype(f32)
+        dp=dotnt(dg[:,sl],vg[:,sl])
+        ds=(pf*(dp-jnp.sum(dp*pf,axis=-1,keepdims=True))).astype(bf)
+        g_ref[hd]+=ds.astype(f32)
+        dqs.append(dot(ds,kg[:,sl])*SCALE)
+        dks.append(dottn(ds,qg[:,sl])*SCALE)
+        dvs.append(dottn(p,dg[:,sl]))
+    for ref,parts in ((dq_ref,dqs),(dk_ref,dks),(dv_ref,dvs)):
+        ref[...]=dot(to_rows,jnp.concatenate(parts,axis=1).astype(bf)).astype(bf)
+    @pl.when(s==pl.num_programs(0)-1)
+    def _():
+        gs_ref[...]=jnp.zeros_like(gs_ref)
+        for hd in range(H):
+            for i in range(SIDE):
+                off=SIDE*(SIDE-1-i)
+                gs_ref[hd,:,off:off+CELLS]+=g_ref[hd,SIDE*i:SIDE*i+SIDE,:]
+
+def attn_bwd(p,do,q,k,v,hw):
+    S=hw.shape[1]; H=q.shape[1]//HD
+    spec=pl.BlockSpec((PAD,H*HD),lambda s:(s,0))
+    o=jax.ShapeDtypeStruct(q.shape,bf)
+    return pl.pallas_call(functools.partial(bwd_kernel,H),grid=(S,),
+        out_shape=(o,o,o,jax.ShapeDtypeStruct((H,SIDE,780),f32)),
+        in_specs=[pl.BlockSpec(memory_space=pltpu.SMEM),pl.BlockSpec((1,H,CELLS,CELLS),lambda s:(s,0,0,0)),spec,spec,spec,spec],
+        out_specs=(spec,spec,spec,pl.BlockSpec((H,SIDE,780),lambda s:(0,0,0))),
+        scratch_shapes=[pltpu.VMEM((H,CELLS,CELLS),f32)],
+        compiler_params=pltpu.CompilerParams(vmem_limit_bytes=48*2**20))(hw,p,do,q,k,v)
+
+def strip_of(table):
+    t=table.reshape(-1,39,39)[:,::-1,::-1]
+    return jnp.stack([t[:,:,19-j:39-j] for j in range(SIDE)],axis=1).reshape(-1,SIDE,780)
+
+def table_of(strip):
+    s=strip.reshape(-1,SIDE,39,SIDE)
+    t=sum(jnp.pad(s[:,j],((0,0),(0,0),(19-j,j))) for j in range(SIDE))
+    return t[:,::-1,::-1].reshape(-1,1521)
 
 
 def layer_norm(values, norm_gain, offset):
@@ -192,45 +311,33 @@
     valid_own = lax.dynamic_slice_in_dim(
         key_valid.reshape(total_rows).astype(jnp.float32), first_own, own_rows, 0
     )
-    rel_index = jax.vmap(grid_index)(grid_height, grid_width)
-    flat_index = rel_index.reshape(-1)
-    side = 2 * GRID_MAX - 1
     time_low = lax.dynamic_index_in_dim(time_embed, group_bucket[0], 0, keepdims=False).astype(
         jnp.bfloat16
     )
     time_f = time_low.astype(jnp.float32)
     share_f = shares.astype(jnp.float32)
     weight = share_f[lax.axis_index("dp")] * share_f.shape[0] / jnp.sum(share_f)
+    hw = jnp.stack([grid_height, grid_width, (slot_ids < group_count[0]).astype(jnp.int32)])
     residual = tokens
-    kept_weights = []
-    layer_pos = 0
     gathered = layer_weights(
-        attend_weight, time_weight, out_weight, expand_weight, reduce_weight, row_params, layer_pos
-    )
-    kept_weights.append(gathered)
+        attend_weight, time_weight, out_weight, expand_weight, reduce_weight, row_params, 0
+    )
     attend_mat, time_mat, out_mat, expand_mat, reduce_mat, rows_mat = gathered
     rows_f = rows_mat.astype(jnp.float32)
-    inputs_kept = [residual]
-    normed = layer_norm(residual, rows_f[0], rows_f[1]).astype(jnp.bfloat16)
-    full_rows = gather_rows(normed)
-    queries, key_rows, values, value_bias = project(full_rows, attend_mat, time_mat, time_low)
-    bias4 = position_bias(bias_table[layer_pos], rel_index)
-    bias_kept = [bias4]
-    scores = score_block(queries, key_rows, bias4, key_valid)
-    top_score = jnp.max(scores, axis=-1, keepdims=True)
-    exponent = jnp.exp(scores - top_score)
-    row_total = jnp.sum(exponent, axis=-1, keepdims=True)
-    lse_kept = [top_score + jnp.log(row_total)]
-    mixed = mix_values((exponent / row_total).astype(jnp.bfloat16), values, value_bias)
+    normed_f, norm_back_one = jax.vjp(layer_norm, residual, rows_f[0], rows_f[1])
+    full_rows_one = gather_rows(normed_f.astype(jnp.bfloat16))
+    queries, key_rows, values, value_bias = project(full_rows_one, attend_mat, time_mat, time_low)
+    mixed, probs = attn_fwd(queries, key_rows, values, strip_of(bias_table[0]), hw)
+    mixed = (mixed + value_bias).astype(jnp.bfloat16)
     residual = residual + spread_sum(partial(rows_product, mixed, out_mat), own_rows) + rows_f[2]
-    middles_kept = [residual]
-    normed = layer_norm(residual, rows_f[3], rows_f[4]).astype(jnp.bfloat16)
-    full_rows = gather_rows(normed)
+    normed_f, norm_back_two = jax.vjp(layer_norm, residual, rows_f[3], rows_f[4])
+    full_rows = gather_rows(normed_f.astype(jnp.bfloat16))
     hidden = (
         jnp.einsum("rd,fd->rf", full_rows, expand_mat, preferred_element_type=jnp.float32)
-        + expand_bias[layer_pos]
-    )
-    activated = gelu_tanh(hidden).astype(jnp.bfloat16)
+        + expand_bias[0]
+    )
+    activated_f, gelu_back = jax.vjp(gelu_tanh, hidden)
+    activated = activated_f.astype(jnp.bfloat16)
     residual = (
         residual + spread_sum(partial(rows_product, activated, reduce_mat), own_rows) + rows_f[5]
     )
@@ -238,25 +345,6 @@
     grad_residual = cotangent * weight * valid_own[:, None]
     results = []
     for layer_pos in reversed(range(LAYERS)):
-        gathered = layer_weights(
-            attend_weight,
-            time_weight,
-            out_weight,
-            expand_weight,
-            reduce_weight,
-            row_params,
-            layer_pos,
-        )
-        attend_mat, time_mat, out_mat, expand_mat, reduce_mat, rows_mat = gathered
-        rows_f = rows_mat.astype(jnp.float32)
-        normed_f, norm_back = jax.vjp(layer_norm, middles_kept[layer_pos], rows_f[3], rows_f[4])
-        full_rows = gather_rows(normed_f.astype(jnp.bfloat16))
-        hidden = (
-            jnp.einsum("rd,fd->rf", full_rows, expand_mat, preferred_element_type=jnp.float32)
-            + expand_bias[layer_pos]
-        )
-        activated_f, gelu_back = jax.vjp(gelu_tanh, hidden)
-        activated = activated_f.astype(jnp.bfloat16)
         grad_full = gather_rows(grad_residual.astype(jnp.bfloat16))
         bias_two = jnp.sum(grad_full.astype(jnp.float32), axis=0)
         grad_reduce = jnp.einsum(
@@ -271,71 +359,20 @@
             "rf,rd->fd", grad_hidden, full_rows, preferred_element_type=jnp.float32
         )
         grad_normed = spread_sum(partial(rows_product, grad_hidden, expand_mat), own_rows)
-        grad_middle, gain_two, offset_two = norm_back(grad_normed)
+        grad_middle, gain_two, offset_two = norm_back_two(grad_normed)
         grad_middle = grad_middle + grad_residual
-        normed_f, norm_back = jax.vjp(layer_norm, inputs_kept[layer_pos], rows_f[0], rows_f[1])
-        full_rows = gather_rows(normed_f.astype(jnp.bfloat16))
-        queries, key_rows, values, value_bias = project(full_rows, attend_mat, time_mat, time_low)
-        scores = score_block(queries, key_rows, bias_kept[layer_pos], key_valid)
-        probs = jnp.exp(scores - lse_kept[layer_pos])
-        weights_low = probs.astype(jnp.bfloat16)
-        mixed = mix_values(weights_low, values, value_bias)
+        full_rows = full_rows_one
+        norm_back = norm_back_one
         grad_full = gather_rows(grad_middle.astype(jnp.bfloat16))
         bias_out = jnp.sum(grad_full.astype(jnp.float32), axis=0)
         grad_out = jnp.einsum("re,rd->ed", mixed, grad_full, preferred_element_type=jnp.float32)
         grad_mixed = jnp.einsum(
             "rd,ed->re", grad_full, out_mat, preferred_element_type=jnp.float32
         ).astype(jnp.bfloat16)
-        shape4 = (SLOTS, PAD, values.shape[1] // HEAD_DIM, HEAD_DIM)
-        grad_mixed4 = grad_mixed.reshape(shape4)
-        grad_probs = jnp.einsum(
-            "sqhe,skhe->shqk",
-            grad_mixed4,
-            values.reshape(shape4),
-            preferred_element_type=jnp.float32,
-        )
-        grad_scores = probs * (grad_probs - jnp.sum(grad_probs * probs, axis=-1, keepdims=True))
-        grad_scores = jnp.where(key_valid[:, None, None, :], grad_scores, 0.0).astype(jnp.bfloat16)
-        grad_table = jax.vmap(
-            lambda plane: jax.ops.segment_sum(
-                plane.reshape(-1), flat_index, num_segments=side * side
-            ),
-            in_axes=1,
-        )(grad_scores.astype(jnp.float32))
-        scale = HEAD_DIM ** (-0.5)
-        grad_queries = (
-            (
-                jnp.einsum(
-                    "shqk,skhe->sqhe",
-                    grad_scores,
-                    key_rows.reshape(shape4),
-                    preferred_element_type=jnp.float32,
-                )
-                * scale
-            )
-            .astype(jnp.bfloat16)
-            .reshape(values.shape)
-        )
-        grad_keys = (
-            (
-                jnp.einsum(
-                    "shqk,sqhe->skhe",
-                    grad_scores,
-                    queries.reshape(shape4),
-                    preferred_element_type=jnp.float32,
-                )
-                * scale
-            )
-            .astype(jnp.bfloat16)
-            .reshape(values.shape)
-        )
-        grad_values = (
-            jnp.einsum(
-                "shqk,sqhe->skhe", weights_low, grad_mixed4, preferred_element_type=jnp.float32
-            )
-            .astype(jnp.bfloat16)
-            .reshape(values.shape)
-        )
+        grad_queries, grad_keys, grad_values, grad_strip = attn_bwd(
+            probs, grad_mixed, queries, key_rows, values, hw
+        )
+        grad_table = table_of(grad_strip)
         grad_triple = jnp.stack([grad_queries, grad_keys, grad_values])
         grad_attend = jnp.einsum(
             "rd,cre->cde", full_rows, grad_triple, preferred_element_type=jnp.float32

time: 4400 us -> 770 us (0.17)
  other arithmetic: 2200 us -> 27 us
  local copies, waits for them, and re-layouts: 1640 us -> 64 us
  waiting for transfers between devices: 347 us -> 478 us
    scatter-add x1 -> x0, other arithmetic: 2170 us -> none  [body(): jax.ops.segment_sum(plane.reshape(-1), flat_index, num_segments=side * side)]
    gather x2 -> x0, local copies, waits for them, and re-layouts: 1470 us -> none  [position_bias(): return jnp.transpose(jnp.take(table, rel_index, axis=1), (1, 0, 2, 3))]
    reshape x7 -> x1, local copies, waits for them, and re-layouts: 105 us -> 0.4 us  [table_of(): s = strip.reshape(-1, SIDE, 39, SIDE)]
    unnamed x17, waiting for transfers between devices: 0.25 us -> 97.9 us
  transfers between devices with their start and end apart: 16 -> 16, of which waited for: 12 -> 14; matrix products, arithmetic and copies ran while one was open for 88% -> 12% of each run, Pallas kernels for 0% -> 0%
where the time goes in v1:
time: 770 us; the launch traced here: 759 us
  waiting for transfers between devices  478 us (62%)
  blocking collectives  79.2 us (10%)
  local copies, waits for them, and re-layouts  64 us (8%)
  matrix products  58.3 us (8%)
  other arithmetic  27 us (4%)
  Pallas kernels  20.4 us (3%)
  between operations  18.4 us (2%)
  starting transfers between devices  14.1 us (2%)
    reduce_scatter x8, waiting for transfers between devices, summed_rows(): subtotal = lax.psum_scatter(subtotal, axis, scatter_dimension=0, tiled=True)  209 us
    all_gather x4, waiting for transfers between devices, gathered_by_axis(): nearer = lax.all_gather(x, axes[-1], axis=dim, tiled=True)  122 us
    unnamed x17, waiting for transfers between devices  97.9 us
    all_gather x4, blocking collectives, gathered_by_axis(): nearer = lax.all_gather(x, axes[-1], axis=dim, tiled=True)  46.6 us
    all_gather x1, waiting for transfers between devices, gather_turned(): filled = lax.all_gather(both, axis, axis=0, tiled=True)  40.9 us
    psum x1, blocking collectives, body(): lax.psum(jnp.stack([gain_one, offset_one, gain_two, offset_two]), MP)  32.7 us
    unnamed x100, local copies, waits for them, and re-layouts  27.2 us
    dot_general x3, matrix products, rows_product(): return jnp.dot(left, right, preferred_element_type=jnp.float32)  16.7 us
  transfers between devices with their start and end apart: 16, of which 14 were waited for; matrix products, arithmetic and copies ran while one was open for 12% of the time, Pallas kernels for 0%

profile of v1, /device:TPU:1, one launch (start us, length us, event | category | flops | bytes accessed | tf_op | source)
XLA Modules:
  0.0 759.1 jit_solution(6495611067241031759)
XLA Ops:
  14.7 40.9 %all-gather.6.cloned.1.call-done = bf16[1152,2022]{1,0:T(8,128)(2,1)} async-done(((bf16[72,2022]{1,0:T(8,128)(2,1)}), bf16[1152,2022]{1,0:T(8,128)(2,1)}) %all-gather.6.cloned.1.call-update) | async-done | bytes 4658704 | tf_op jit(solution)/shard_map/all_gather | solution.py:43
  58.7 12.2 %all_gather.28 = bf16[320,1152]{1,0:T(8,128)(2,1)} all-gather(bf16[160,1152]{1,0:T(8,128)(2,1)S(1)} %add_convert_fusion.2), channel_id=1, replica_groups=mesh['dp'=16,'mp_0'=4,'mp_1'=2] {'mp_1'}, dimensions={0}, use_global_device_ids=true | all-gather | bytes 1105920 | tf_op jit(solution)/shard_map/all_gather | solution.py:28
  82.6 26.9 %all-gather.8.cloned.1.call-done = bf16[1280,1152]{1,0:T(8,128)(2,1)} async-done(((bf16[320,1152]{1,0:T(8,128)(2,1)}), bf16[1280,1152]{1,0:T(8,128)(2,1)}) %all-gather.8.cloned.1.call-update) | async-done | bytes 2949136 | tf_op jit(solution)/shard_map/all_gather | solution.py:28
  115.2 8.6 %shard_map.231 = (f32[1280,144]{1,0:T(8,128)S(1)}, bf16[4,2,400,400]{3,2,1,0:T(8,128)(2,1)}) custom-call(s32[3,4]{1,0:T(4,128)S(1)} %pad_add_fusion.1.hw_ref, f32[2,20,780]{2,1,0:T(8,128)S(1)} %copy-done.1, bf16[1280,144]{1,0:T(8,128)(2,1)S(1)} %fusion.18.q_ref, bf16[1280,144]{1,0:T(8,128)(2,1)S(1)} %get-tuple-element.91.k_ref, ...), custom_call_target="tpu_custom_call" | custom-call | tf_op jit(solution)/shard_map/pallas_call | solution.py:135
  127.0 36.7 %reduce-scatter.13.cloned.1.call-done = bf16[320,1152]{1,0:T(8,128)(2,1)} async-done(((bf16[1280,1152]{1,0:T(8,128)(2,1)}), bf16[320,1152]{1,0:T(8,128)(2,1)}) %reduce-scatter.13.cloned.1.call-update) | async-done | bytes 737296 | tf_op jit(solution)/shard_map/reduce_scatter | solution.py:35
  163.8 23.0 %reduce-scatter.15.cloned.1.call-done = bf16[160,1152]{1,0:T(8,128)(2,1)} async-done(((bf16[320,1152]{1,0:T(8,128)(2,1)}), bf16[160,1152]{1,0:T(8,128)(2,1)}) %reduce-scatter.15.cloned.1.call-update) | async-done | bytes 368656 | tf_op jit(solution)/shard_map/reduce_scatter | solution.py:35
  189.2 11.8 %all_gather.30 = bf16[320,1152]{1,0:T(8,128)(2,1)} all-gather(bf16[160,1152]{1,0:T(8,128)(2,1)S(1)} %add_convert_fusion.1), channel_id=1, replica_groups=mesh['dp'=16,'mp_0'=4,'mp_1'=2] {'mp_1'}, dimensions={0}, use_global_device_ids=true | all-gather | bytes 1105920 | tf_op jit(solution)/shard_map/all_gather | solution.py:28
  205.1 10.9 %all_gather.32 = bf16[320,1152]{1,0:T(8,128)(2,1)} all-gather(bf16[160,1152]{1,0:T(8,128)(2,1)S(1)} %fusion.34), channel_id=1, replica_groups=mesh['dp'=16,'mp_0'=4,'mp_1'=2] {'mp_1'}, dimensions={0}, use_global_device_ids=true | all-gather | bytes 1105920 | tf_op jit(solution)/shard_map/all_gather | solution.py:28
  216.1 23.2 %all-gather.10.cloned.1.call-done = bf16[1280,1152]{1,0:T(8,128)(2,1)} async-done(((bf16[320,1152]{1,0:T(8,128)(2,1)}), bf16[1280,1152]{1,0:T(8,128)(2,1)}) %all-gather.10.cloned.1.call-update) | async-done | bytes 2949136 | tf_op jit(solution)/shard_map/all_gather | solution.py:28
  245.7 33.3 %all-gather.12.cloned.1.call-done = bf16[1280,1152]{1,0:T(8,128)(2,1)} async-done(((bf16[320,1152]{1,0:T(8,128)(2,1)}), bf16[1280,1152]{1,0:T(8,128)(2,1)}) %all-gather.12.cloned.1.call-update) | async-done | bytes 2949136 | tf_op jit(solution)/shard_map/all_gather | solution.py:28
  279.0 8.0 %convert_reduce_fusion = (f32[576]{0:T(1024)}, bf16[1280,576]{0,1:T(8,128)(2,1)S(1)}) fusion(f32[1280,576]{0,1:T(8,128)} %convolution_add_fusion, bf16[1280,1152]{1,0:T(8,128)(2,1)} %all-gather.12.cloned.1.call-done, bf16[1152,2022]{1,0:T(8,128)(2,1)} %all-gather.6.cloned.1.call-done), kind=kOutput, calls=%fused_computation.21 | convolution fusion | flops 1714912768 | bytes 8849664 | tf_op jit(solution)/shard_map/rd,fd->rf/dot_general | solution.py:353
  302.6 29.0 %reduce-scatter.21.cloned.1.call-done = bf16[320,1152]{1,0:T(8,128)(2,1)} async-done(((bf16[1280,1152]{1,0:T(8,128)(2,1)}), bf16[320,1152]{1,0:T(8,128)(2,1)}) %reduce-scatter.21.cloned.1.call-update) | async-done | bytes 737296 | tf_op jit(solution)/shard_map/reduce_scatter | solution.py:35
  331.7 38.7 %reduce-scatter.17.cloned.1.call-done = bf16[320,1152]{1,0:T(8,128)(2,1)} async-done(((bf16[1280,1152]{1,0:T(8,128)(2,1)}), bf16[320,1152]{1,0:T(8,128)(2,1)}) %reduce-scatter.17.cloned.1.call-update) | async-done | bytes 737296 | tf_op jit(solution)/shard_map/reduce_scatter | solution.py:35
  370.5 23.1 %reduce-scatter.23.cloned.1.call-done = bf16[160,1152]{1,0:T(8,128)(2,1)} async-done(((bf16[320,1152]{1,0:T(8,128)(2,1)}), bf16[160,1152]{1,0:T(8,128)(2,1)}) %reduce-scatter.23.cloned.1.call-update) | async-done | bytes 368656 | tf_op jit(solution)/shard_map/reduce_scatter | solution.py:35
  395.2 21.2 %reduce-scatter.19.cloned.1.call-done = bf16[160,1152]{1,0:T(8,128)(2,1)} async-done(((bf16[320,1152]{1,0:T(8,128)(2,1)}), bf16[160,1152]{1,0:T(8,128)(2,1)}) %reduce-scatter.19.cloned.1.call-update) | async-done | bytes 368656 | tf_op jit(solution)/shard_map/reduce_scatter | solution.py:35
  419.9 11.7 %all_gather.34 = bf16[320,1152]{1,0:T(8,128)(2,1)} all-gather(bf16[160,1152]{1,0:T(8,128)(2,1)S(1)} %fusion.52), channel_id=1, replica_groups=mesh['dp'=16,'mp_0'=4,'mp_1'=2] {'mp_1'}, dimensions={0}, use_global_device_ids=true | all-gather | bytes 1105920 | tf_op jit(solution)/shard_map/all_gather | solution.py:28
  431.7 38.3 %all-gather.14.cloned.1.call-done = bf16[1280,1152]{1,0:T(8,128)(2,1)} async-done(((bf16[320,1152]{1,0:T(8,128)(2,1)}), bf16[1280,1152]{1,0:T(8,128)(2,1)}) %all-gather.14.cloned.1.call-update) | async-done | bytes 2949136 | tf_op jit(solution)/shard_map/all_gather | solution.py:28
  473.1 11.8 %shard_map.232 = (bf16[1280,144]{1,0:T(8,128)(2,1)S(1)}, bf16[1280,144]{1,0:T(8,128)(2,1)S(1)}, bf16[1280,144]{1,0:T(8,128)(2,1)S(1)}, f32[2,20,780]{2,1,0:T(8,128)S(1)}) custom-call(s32[3,4]{1,0:T(4,128)S(1)} %pad_add_fusion.1.hw_ref, bf16[4,2,400,400]{3,2,1,0:T(8,128)(2,1)} %get-tuple-element.17.p_ref, bf16[1280,144]{1,0:T(8,128)(2,1)S(1)} %get-tuple-element.138.do_ref, ...), custom_call_target="tpu_custom_call" | custom-call | tf_op jit(solution)/shard_map/pallas_call | solution.py:178
  490.7 36.9 %reduce-scatter.25.cloned.1.call-done = bf16[320,1152]{1,0:T(8,128)(2,1)} async-done(((bf16[1280,1152]{1,0:T(8,128)(2,1)}), bf16[320,1152]{1,0:T(8,128)(2,1)}) %reduce-scatter.25.cloned.1.call-update) | async-done | bytes 737296 | tf_op jit(solution)/shard_map/reduce_scatter | solution.py:35
  567.1 32.7 %psum.7 = bf16[4,1152]{1,0:T(4,128)(2,1)S(1)} all-reduce(f32[4,1152]{1,0:T(4,128)S(1)} %pad_maximum_fusion.4), channel_id=1, replica_groups=mesh['dp'=16,'mp_0'=4,'mp_1'=2] {'mp_0','mp_1'}, use_global_device_ids=true, to_apply=%region_24.25 | all-reduce | flops 4608 | bytes 27648 | tf_op jit(solution)/shard_map/psum | solution.py:389
  599.8 13.9 %concatenate.17 = bf16[1302,1152]{1,0:T(8,128)(2,1)} concatenate(bf16[144,1152]{1,0:T(8,128)(2,1)} %convolution_convert_fusion.6, bf16[576,1152]{1,0:T(8,128)(2,1)S(1)} %convolution_convert_fusion.4, bf16[576,1152]{1,0:T(8,128)(2,1)} %convolution_convert_fusion.3, bf16[2,1152]{1,0:T(2,128)(2,1)S(1)} %get-tuple-element.132, bf16[1,1152]{1,0:T(2,128)(2,1)S(1)} %stack.179, ...), dimensions={0} | concatenate | bytes 5999616 | tf_op jit(solution)/shard_map/concatenate | solution.py:54
  620.2 12.7 %all-to-all-start = ((f32[16,1,3618]{2,1,0:T(1,128)}), f32[16,1,3618]{2,1,0:T(1,128)S(1)}, u32[]{:S(2)}, u32[]{:S(2)}) async-start(f32[16,1,3618]{2,1,0:T(1,128)} %broadcast_in_dim.14), calls=%async_computation.8 | async-start | bytes 475136 | tf_op jit(solution)/shard_map/all_to_all | solution.py:64
  634.2 8.6 %all-to-all-done = f32[16,1,3618]{2,1,0:T(1,128)S(1)} async-done(((f32[16,1,3618]{2,1,0:T(1,128)}), f32[16,1,3618]{2,1,0:T(1,128)S(1)}, u32[]{:S(2)}, u32[]{:S(2)}) %all-to-all-start) | async-done | bytes 231584 | tf_op jit(solution)/shard_map/all_to_all | solution.py:64
  648.9 97.6 %all-reduce.23.cloned.1.call-done = bf16[1302,1152]{1,0:T(8,128)(2,1)} async-done(((bf16[1302,1152]{1,0:T(8,128)(2,1)}), bf16[1302,1152]{1,0:T(8,128)(2,1)}) %all-reduce.23.cloned.1.call-update) | async-done | bytes 2999824
  (269 shorter events, 129.0 us)
Async XLA Ops:
  7.2 75.0 %copy-start = (f32[32,1152]{1,0:T(8,128)S(1)}, f32[32,1152]{1,0:T(8,128)}, u32[]{:S(2)}) copy-start(f32[32,1152]{1,0:T(8,128)} %param.18) | copy-start | bytes 442372
  7.2 48.3 %all-gather.6.cloned.1.call-start = ((), (), s32[]{:S(2)}) async-start(), calls=%async_computation.10 | async-start | bytes 5013504 | tf_op jit(solution)/shard_map/all_gather | solution.py:43
  13.1 96.4 %all-gather.8.cloned.1.call-start = ((), (), s32[]{:S(2)}) async-start(), calls=%async_computation.11 | async-start | bytes 3686400 | tf_op jit(solution)/shard_map/all_gather | solution.py:28
  14.6 40.9 %copy-start.30 = (f32[160]{0:T(256)}, f32[160]{0:T(256)S(1)}, u32[]{:S(2)}) copy-start(f32[160]{0:T(256)S(1)} %multiply_reduce_fusion.1) | copy-start | bytes 1924
  14.6 56.2 %copy-start.23 = (f32[160]{0:T(256)}, f32[160]{0:T(256)S(1)}, u32[]{:S(2)}) copy-start(f32[160]{0:T(256)S(1)} %fusion.48) | copy-start | bytes 1924
  70.9 92.8 %reduce-scatter.13.cloned.1.call-start = ((), (), s32[]{:S(2)}) async-start(), calls=%async_computation.12 | async-start | bytes 3686400 | tf_op jit(solution)/shard_map/reduce_scatter | solution.py:35
  82.4 41.4 %copy-start.33 = (f32[1,144]{1,0:T(1,128)}, f32[1,144]{1,0:T(1,128)S(1)}, u32[]{:S(2)}) copy-start(f32[1,144]{1,0:T(1,128)S(1)} %fusion.37) | copy-start | bytes 1732
  126.7 60.0 %reduce-scatter.15.cloned.1.call-start = ((), (), s32[]{:S(2)}) async-start(), calls=%async_computation.13 | async-start | bytes 1105920 | tf_op jit(solution)/shard_map/reduce_scatter | solution.py:35
  163.7 75.6 %all-gather.10.cloned.1.call-start = ((), (), s32[]{:S(2)}) async-start(), calls=%async_computation.14 | async-start | bytes 3686400 | tf_op jit(solution)/shard_map/all_gather | solution.py:28
  201.0 78.0 %all-gather.12.cloned.1.call-start = ((), (), s32[]{:S(2)}) async-start(), calls=%async_computation.17 | async-start | bytes 3686400 | tf_op jit(solution)/shard_map/all_gather | solution.py:28
  216.0 115.6 %reduce-scatter.21.cloned.1.call-start = ((), (), s32[]{:S(2)}) async-start(), calls=%async_computation.18 | async-start | bytes 3686400 | tf_op jit(solution)/shard_map/reduce_scatter | solution.py:35
  294.6 75.8 %reduce-scatter.17.cloned.1.call-start = ((), (), s32[]{:S(2)}) async-start(), calls=%async_computation.15 | async-start | bytes 3686400 | tf_op jit(solution)/shard_map/reduce_scatter | solution.py:35
  302.5 91.1 %reduce-scatter.23.cloned.1.call-start = ((), (), s32[]{:S(2)}) async-start(), calls=%async_computation.19 | async-start | bytes 1105920 | tf_op jit(solution)/shard_map/reduce_scatter | solution.py:35
  331.6 84.7 %reduce-scatter.19.cloned.1.call-start = ((), (), s32[]{:S(2)}) async-start(), calls=%async_computation.16 | async-start | bytes 1105920 | tf_op jit(solution)/shard_map/reduce_scatter | solution.py:35
  370.4 99.5 %all-gather.14.cloned.1.call-start = ((), (), s32[]{:S(2)}) async-start(), calls=%async_computation.20 | async-start | bytes 3686400 | tf_op jit(solution)/shard_map/all_gather | solution.py:28
  419.0 54.1 %copy-start.26 = (f32[160]{0:T(256)}, f32[160]{0:T(256)S(1)}, u32[]{:S(2)}) copy-start(f32[160]{0:T(256)S(1)} %negate_multiply_fusion.1) | copy-start | bytes 1924
  431.6 96.1 %reduce-scatter.25.cloned.1.call-start = ((), (), s32[]{:S(2)}) async-start(), calls=%async_computation.21 | async-start | bytes 3686400 | tf_op jit(solution)/shard_map/reduce_scatter | solution.py:35
  490.6 37.7 %copy-start.7 = (bf16[1280,144]{1,0:T(8,128)(2,1)S(1)}, bf16[1280,144]{1,0:T(8,128)(2,1)}, u32[]{:S(2)}) copy-start(bf16[1280,144]{1,0:T(8,128)(2,1)} %copy-done.6) | copy-start | bytes 1105924
  490.7 37.7 %copy-start.9 = (bf16[1280,144]{1,0:T(8,128)(2,1)S(1)}, bf16[1280,144]{1,0:T(8,128)(2,1)}, u32[]{:S(2)}) copy-start(bf16[1280,144]{1,0:T(8,128)(2,1)} %copy-done.8) | copy-start | bytes 1105924
  490.7 71.8 %reduce-scatter.27.cloned.1.call-start = ((), (), s32[]{:S(2)}) async-start(), calls=%async_computation.22 | async-start | bytes 1105920 | tf_op jit(solution)/shard_map/reduce_scatter | solution.py:35
  527.7 116.6 %reduce-scatter.29.cloned.1.call-start = ((), (), s32[]{:S(2)}) async-start(), calls=%async_computation.23 | async-start | bytes 1880064
  544.4 202.1 %all-reduce.23.cloned.1.call-start = ((), (), s32[]{:S(2)}) async-start(), calls=%async_computation.24 | async-start | bytes 6008832
  559.1 40.7 %copy-start.22 = (bf16[1,1152]{1,0:T(2,128)(2,1)S(1)}, bf16[1,1152]{1,0:T(2,128)(2,1)}, u32[]{:S(2)}) copy-start(bf16[1,1152]{1,0:T(2,128)(2,1)} %stack.180) | copy-start | bytes 6916
  620.2 22.5 %all-to-all-start = ((f32[16,1,3618]{2,1,0:T(1,128)}), f32[16,1,3618]{2,1,0:T(1,128)S(1)}, u32[]{:S(2)}, u32[]{:S(2)}) async-start(f32[16,1,3618]{2,1,0:T(1,128)} %broadcast_in_dim.14), calls=%async_computation.8 | async-start | bytes 475136 | tf_op jit(solution)/shard_map/all_to_all | solution.py:64
  (36 other events, 516.4 us)
Sparse Core Ops, SparseCore 0:
  13.2 42.2 all-gather.5
  71.0 38.4 all-gather.7
  126.8 36.8 reduce-scatter.12
  166.0 20.6 reduce-scatter.14
  201.1 38.1 all-gather.9
  240.9 38.0 all-gather.11
  294.7 36.8 reduce-scatter.20
  334.0 36.3 reduce-scatter.16
  372.9 20.6 reduce-scatter.22
  395.9 20.3 reduce-scatter.18
  431.7 38.1 all-gather.13
  490.8 36.8 reduce-scatter.24
  530.0 20.6 reduce-scatter.26
  553.0 60.4 reduce-scatter.28
  616.0 130.4 all-reduce.22
